TPU v7x, 256 devices: a whole 4x4x8 slice. The times are simulated.
256 devices in a mesh: dp: 8 (over y, z_lo), context: 32 (over x, z_hi, core).
Axes of the slice: x: 4, y: 4, z: 8 (z_hi: 4, z_lo: 2; z = z_hi * 2 + z_lo), core: 2. Of those that a mesh axis runs over, the one named last changes fastest.
Arguments:
- query_rows: bfloat16 [32768, 4096], P(('dp', 'context')), parts along dimension 0, may hold values from -6 to 6
- key_rows: bfloat16 [32768, 512], P(('dp', 'context')), parts along dimension 0, may hold values from -6 to 6
- value_rows: bfloat16 [32768, 512], P(('dp', 'context')), parts along dimension 0, may hold values from -6 to 6
- grad_out: bfloat16 [32768, 4096], P(('dp', 'context')), parts along dimension 0, may hold values from -6 to 6
- doc_bounds: int32 [72], P('dp'), parts along dimension 0, may hold values from 0 to 4096, as said below
Outputs:
- attn_out: bfloat16 [32768, 4096], P(('dp', 'context')), parts along dimension 0
- d_query: bfloat16 [32768, 4096], P(('dp', 'context')), parts along dimension 0
- d_key: bfloat16 [32768, 512], P(('dp', 'context')), parts along dimension 0
- d_value: bfloat16 [32768, 512], P(('dp', 'context')), parts along dimension 0
There are 8 independent parts, one for each index of `dp`. A program takes and returns all parts, laid end to end along the dimension named above; each array names one. Nothing has to cross between parts.
Inputs may be any that keep to these rules, and one draw needn't show every extreme that they name: doc_bounds[0] = 0, doc_bounds[8] = 4096, strictly rising; every response is 256 to 1024 tokens long; at least one is exactly 1024 and at least one exactly 256.
All inputs are finite; a program needn't handle non-finite values.
Results may differ from a plain program's by a relative error of at most 0.035.
Values may be sent and summed in bfloat16 or wider, within the bound.
A program may use at most 64 MiB of HBM per device.

v0:
```python
import jax
import jax.numpy as jnp
from jax import lax
from jax.sharding import PartitionSpec as P

HEAD_DIM = 128
MAXDOC = 1024
QBLOCK = 512


masked_score = -1e30


def segment_ids(positions, doc_bounds):
    inner_bounds = doc_bounds[1:-1]
    return jnp.sum((positions[:, None] >= inner_bounds[None, :]).astype(jnp.int32), axis=1)


def block_pass(q_block, k_window, v_window, o_grad, allowed, softmax_scale):
    scores = (
        jnp.einsum("qhd,kd->hqk", q_block, k_window, preferred_element_type=jnp.float32)
        * softmax_scale
    )
    scores = jnp.where(allowed[None], scores, masked_score)
    top_score = jnp.max(scores, axis=-1, keepdims=True)
    expd = jnp.where(allowed[None], jnp.exp(scores - top_score), 0.0)
    probs = expd / jnp.sum(expd, axis=-1, keepdims=True)
    weights = probs.astype(jnp.bfloat16)
    attended = jnp.einsum(
        "hqk,kd->qhd", weights, v_window, preferred_element_type=jnp.float32
    ).astype(jnp.bfloat16)
    inner_prod = jnp.sum(o_grad.astype(jnp.float32) * attended.astype(jnp.float32), axis=-1)
    prob_grad = jnp.einsum("qhd,kd->hqk", o_grad, v_window, preferred_element_type=jnp.float32)
    score_grad = (probs * (prob_grad - jnp.transpose(inner_prod)[:, :, None])).astype(jnp.bfloat16)
    q_grad = (
        softmax_scale
        * jnp.einsum("hqk,kd->qhd", score_grad, k_window, preferred_element_type=jnp.float32)
    ).astype(jnp.bfloat16)
    k_grad = softmax_scale * jnp.einsum(
        "hqk,qhd->kd", score_grad, q_block, preferred_element_type=jnp.float32
    )
    v_grad = jnp.einsum("hqk,qhd->kd", weights, o_grad, preferred_element_type=jnp.float32)
    return (attended, q_grad, k_grad, v_grad)


def head_pass(q_heads, k_head, v_head, g_heads, doc_bounds, softmax_scale):
    length = q_heads.shape[0]
    width = k_head.shape[1]
    span = QBLOCK + MAXDOC
    k_pad = jnp.concatenate([jnp.zeros((MAXDOC, width), k_head.dtype), k_head], axis=0)
    v_pad = jnp.concatenate([jnp.zeros((MAXDOC, width), v_head.dtype), v_head], axis=0)
    seg_all = segment_ids(jnp.arange(length + MAXDOC, dtype=jnp.int32) - MAXDOC, doc_bounds)

    def step(carry, start):
        k_acc, v_acc = carry
        q_block = lax.dynamic_slice_in_dim(q_heads, start, QBLOCK, 0)
        g_block = lax.dynamic_slice_in_dim(g_heads, start, QBLOCK, 0)
        k_window = lax.dynamic_slice_in_dim(k_pad, start, span, 0)
        v_window = lax.dynamic_slice_in_dim(v_pad, start, span, 0)
        q_pos = start + jnp.arange(QBLOCK, dtype=jnp.int32)
        k_pos = start - MAXDOC + jnp.arange(span, dtype=jnp.int32)
        q_seg = lax.dynamic_slice_in_dim(seg_all, start + MAXDOC, QBLOCK, 0)
        k_seg = lax.dynamic_slice_in_dim(seg_all, start, span, 0)
        allowed = (
            (q_seg[:, None] == k_seg[None, :])
            & (k_pos[None, :] <= q_pos[:, None])
            & (k_pos[None, :] >= 0)
        )
        attended, q_grad, k_grad, v_grad = block_pass(
            q_block, k_window, v_window, g_block, allowed, softmax_scale
        )
        k_acc = lax.dynamic_update_slice_in_dim(
            k_acc, lax.dynamic_slice_in_dim(k_acc, start, span, 0) + k_grad, start, 0
        )
        v_acc = lax.dynamic_update_slice_in_dim(
            v_acc, lax.dynamic_slice_in_dim(v_acc, start, span, 0) + v_grad, start, 0
        )
        return ((k_acc, v_acc), (attended, q_grad))

    starts = jnp.arange(0, length, QBLOCK, dtype=jnp.int32)
    empty = jnp.zeros((length + MAXDOC, width), jnp.float32)
    (k_acc, v_acc), (attended, q_grad) = lax.scan(step, (empty, empty), starts)
    heads_here = q_heads.shape[1]
    return (
        attended.reshape(length, heads_here, width),
        q_grad.reshape(length, heads_here, width),
        k_acc[MAXDOC:],
        v_acc[MAXDOC:],
    )


def body(query_rows, key_rows, value_rows, grad_out, doc_bounds):
    tok_rows = query_rows.shape[0]
    width = HEAD_DIM
    kv_count = key_rows.shape[1] // width
    softmax_scale = HEAD_DIM ** (-0.5)
    devices = lax.axis_size("context")
    per_slot = devices // kv_count
    k_slots = jnp.broadcast_to(
        key_rows.reshape(tok_rows, kv_count, 1, width), (tok_rows, kv_count, per_slot, width)
    ).reshape(tok_rows, devices * width)
    v_slots = jnp.broadcast_to(
        value_rows.reshape(tok_rows, kv_count, 1, width), (tok_rows, kv_count, per_slot, width)
    ).reshape(tok_rows, devices * width)
    q_cols, k_cols, v_cols, g_cols = (
        lax.all_to_all(query_rows, "context", split_axis=1, concat_axis=0, tiled=True),
        lax.all_to_all(k_slots, "context", split_axis=1, concat_axis=0, tiled=True),
        lax.all_to_all(v_slots, "context", split_axis=1, concat_axis=0, tiled=True),
        lax.all_to_all(grad_out, "context", split_axis=1, concat_axis=0, tiled=True),
    )
    length = q_cols.shape[0]
    heads_here = q_cols.shape[1] // width
    attended, q_grad, k_grad, v_grad = head_pass(
        q_cols.reshape(length, heads_here, width),
        k_cols,
        v_cols,
        g_cols.reshape(length, heads_here, width),
        doc_bounds,
        softmax_scale,
    )
    attn_out, d_query = (
        lax.all_to_all(
            attended.reshape(length, heads_here * width),
            "context",
            split_axis=0,
            concat_axis=1,
            tiled=True,
        ),
        lax.all_to_all(
            q_grad.reshape(length, heads_here * width),
            "context",
            split_axis=0,
            concat_axis=1,
            tiled=True,
        ),
    )
    k_back, v_back = (
        lax.all_to_all(
            k_grad.astype(jnp.bfloat16), "context", split_axis=0, concat_axis=1, tiled=True
        ).astype(k_grad.dtype),
        lax.all_to_all(
            v_grad.astype(jnp.bfloat16), "context", split_axis=0, concat_axis=1, tiled=True
        ).astype(v_grad.dtype),
    )
    d_key = (
        k_back.reshape(tok_rows, kv_count, per_slot, width)
        .sum(axis=2)
        .reshape(tok_rows, kv_count * width)
    )
    d_value = (
        v_back.reshape(tok_rows, kv_count, per_slot, width)
        .sum(axis=2)
        .reshape(tok_rows, kv_count * width)
    )
    return (attn_out, d_query, d_key.astype(jnp.bfloat16), d_value.astype(jnp.bfloat16))


def solution(mesh):
    return jax.shard_map(
        body,
        mesh=mesh,
        in_specs=(
            P(("dp", "context"), None),
            P(("dp", "context"), None),
            P(("dp", "context"), None),
            P(("dp", "context"), None),
            P("dp"),
        ),
        out_specs=(
            P(("dp", "context"), None),
            P(("dp", "context"), None),
            P(("dp", "context"), None),
            P(("dp", "context"), None),
        ),
        check_vma=False,
    )
```

profile of v0, /device:TPU:1, one launch (start us, length us, event | category | flops | bytes accessed | tf_op | source)
XLA Modules:
  0.0 593.7 jit_solution(18121531770683114527)
XLA Ops:
  2.8 12.6 %all-to-all-start.2 = ((bf16[128,32,128]{2,0,1:T(8,128)(2,1)}), bf16[128,32,128]{2,0,1:T(8,128)(2,1)S(1)}, u32[]{:S(2)}, u32[]{:S(2)}) async-start(bf16[128,32,128]{2,0,1:T(8,128)(2,1)} %bitcast.22), calls=%async_computation.2 | async-start | bytes 2097152 | tf_op jit(solution)/shard_map/all_to_all | solution.py:108
  15.4 28.9 %all-to-all-done.2 = bf16[128,32,128]{2,0,1:T(8,128)(2,1)S(1)} async-done(((bf16[128,32,128]{2,0,1:T(8,128)(2,1)}), bf16[128,32,128]{2,0,1:T(8,128)(2,1)S(1)}, u32[]{:S(2)}, u32[]{:S(2)}) %all-to-all-start.2) | async-done | bytes 1048608 | tf_op jit(solution)/shard_map/all_to_all | solution.py:108
  45.5 5.3 all-to-all-start
  52.1 27.1 %all-to-all-done = bf16[128,32,128]{2,0,1:T(8,128)(2,1)S(1)} async-done(((bf16[128,32,128]{2,0,1:T(8,128)(2,1)}), bf16[128,32,128]{2,0,1:T(8,128)(2,1)S(1)}, u32[]{:S(2)}, u32[]{:S(2)}) %all-to-all-start) | async-done | bytes 1048608 | tf_op jit(solution)/shard_map/all_to_all | solution.py:107
  79.2 6.1 %all-to-all-start.1 = ((bf16[128,32,128]{0,2,1:T(8,128)(2,1)}), bf16[128,32,128]{0,2,1:T(8,128)(2,1)S(1)}, u32[]{:S(2)}, u32[]{:S(2)}) async-start(bf16[128,32,128]{0,2,1:T(8,128)(2,1)} %bitcast.147), calls=%async_computation.1 | async-start | bytes 2097152 | tf_op jit(solution)/shard_map/all_to_all | solution.py:106
  87.6 27.1 %all-to-all-done.1 = bf16[128,32,128]{0,2,1:T(8,128)(2,1)S(1)} async-done(((bf16[128,32,128]{0,2,1:T(8,128)(2,1)}), bf16[128,32,128]{0,2,1:T(8,128)(2,1)S(1)}, u32[]{:S(2)}, u32[]{:S(2)}) %all-to-all-start.1) | async-done | bytes 1048608 | tf_op jit(solution)/shard_map/all_to_all | solution.py:106
  114.7 4.9 all-to-all-start.3
  123.7 24.4 %all-to-all-done.3 = bf16[128,32,128]{0,2,1:T(8,128)(2,1)} async-done(((bf16[128,32,128]{0,2,1:T(8,128)(2,1)}), bf16[128,32,128]{0,2,1:T(8,128)(2,1)}, u32[]{:S(2)}, u32[]{:S(2)}) %all-to-all-start.3) | async-done | bytes 1048608 | tf_op jit(solution)/shard_map/all_to_all | solution.py:109
  153.7 302.3 %while.18 = (s32[]{:T(128)}, f32[5120,128]{1,0:T(8,128)}, f32[5120,128]{1,0:T(8,128)}, bf16[8,512,1,128]{3,1,0,2:T(8,128)(2,1)}, bf16[8,512,1,128]{3,1,0,2:T(8,1...) while((s32[]{:T(128)}, f32[5120,128]{1,0:T(8,128)}, ...), condition=%wide.region_5.6_spmd, body=%wide.region_1.5_spmd.sunk | while | flops 1240468992 | bytes 34337328 | solution.py:82
  163.0 3.2 fusion.63
  168.0 3.8 multiply_reduce_fusion.2
  172.9 4.5 convolution_add_fusion.2
  177.4 3.0 fusion.65
  184.7 3.5 dynamic_update_slice.31
  188.1 3.5 dynamic_update_slice.32
  200.9 3.2 fusion.63
  205.9 3.8 multiply_reduce_fusion.2
  210.8 4.5 convolution_add_fusion.2
  215.4 3.0 fusion.65
  222.6 3.5 dynamic_update_slice.31
  226.1 3.5 dynamic_update_slice.32
  238.9 3.2 fusion.63
  243.8 3.8 multiply_reduce_fusion.2
  248.7 4.5 convolution_add_fusion.2
  253.3 3.0 fusion.65
  260.5 3.5 dynamic_update_slice.31
  264.0 3.5 dynamic_update_slice.32
  276.8 3.2 fusion.63
  281.7 3.8 multiply_reduce_fusion.2
  286.6 4.5 convolution_add_fusion.2
  291.2 3.0 fusion.65
  298.4 3.5 dynamic_update_slice.31
  301.9 3.5 dynamic_update_slice.32
  314.7 3.2 fusion.63
  319.6 3.8 multiply_reduce_fusion.2
  324.6 4.5 convolution_add_fusion.2
  329.1 3.0 fusion.65
  336.3 3.5 dynamic_update_slice.31
  339.8 3.5 dynamic_update_slice.32
  352.7 3.2 fusion.63
  357.6 3.8 multiply_reduce_fusion.2
  362.5 4.5 convolution_add_fusion.2
  367.1 3.0 fusion.65
  374.3 3.5 dynamic_update_slice.31
  377.8 3.5 dynamic_update_slice.32
  390.6 3.2 fusion.63
  395.5 3.8 multiply_reduce_fusion.2
  400.4 4.5 convolution_add_fusion.2
  405.0 3.0 fusion.65
  412.2 3.5 dynamic_update_slice.31
  415.7 3.5 dynamic_update_slice.32
  428.5 3.2 fusion.63
  433.4 3.8 multiply_reduce_fusion.2
  438.4 4.5 convolution_add_fusion.2
  442.9 3.0 fusion.65
  450.1 3.0 dynamic_update_slice.31
  453.1 3.0 dynamic_update_slice.32
  456.0 34.0 %all_to_all.134 = bf16[32,128,128]{2,1,0:T(8,128)(2,1)S(1)} all-to-all(bf16[32,128,128]{2,1,0:T(8,128)(2,1)} %bitcast.152), channel_id=1, replica_groups=mesh['dp'=8,'context'=32] {'context'}, dimensions={0} | all-to-all | bytes 2097152 | tf_op jit(solution)/shard_map/all_to_all | solution.py:129
  490.0 4.5 all-to-all-start.4
  497.2 26.6 %all-to-all-done.4 = bf16[32,128,128]{2,1,0:T(8,128)(2,1)S(1)} async-done(((bf16[32,128,128]{2,1,0:T(8,128)(2,1)}), bf16[32,128,128]{2,1,0:T(8,128)(2,1)S(1)}, u32[]{:S(2)}, u32[]{:S(2)}) %all-to-all-start.4) | async-done | bytes 1048608 | tf_op jit(solution)/shard_map/all_to_all | solution.py:122
  523.7 4.8 all-to-all-start.6
  531.2 26.1 %all-to-all-done.6 = bf16[32,128,128]{2,1,0:T(8,128)(2,1)S(1)} async-done(((bf16[32,128,128]{2,1,0:T(8,128)(2,1)}), bf16[32,128,128]{2,1,0:T(8,128)(2,1)S(1)}, u32[]{:S(2)}, u32[]{:S(2)}) %all-to-all-start.6) | async-done | bytes 1048608 | tf_op jit(solution)/shard_map/all_to_all | solution.py:138
  557.3 4.7 all-to-all-start.7
  568.6 22.7 %all-to-all-done.7 = bf16[32,128,128]{2,1,0:T(8,128)(2,1)} async-done(((bf16[32,128,128]{2,1,0:T(8,128)(2,1)}), bf16[32,128,128]{2,1,0:T(8,128)(2,1)}, u32[]{:S(2)}, u32[]{:S(2)}) %all-to-all-start.7) | async-done | bytes 1048608 | tf_op jit(solution)/shard_map/all_to_all | solution.py:141
  (406 shorter events, 118.2 us)
Async XLA Ops:
  0.6 14.7 %copy-start.11 = (bf16[128,512]{1,0:T(8,128)(2,1)S(1)}, bf16[128,512]{1,0:T(8,128)(2,1)}, u32[]{:S(2)}) copy-start(bf16[128,512]{1,0:T(8,128)(2,1)} %param.8) | copy-start | bytes 393220
  1.6 49.2 %copy-start.2 = (bf16[128,4096]{1,0:T(8,128)(2,1)S(1)}, bf16[128,4096]{1,0:T(8,128)(2,1)}, u32[]{:S(2)}) copy-start(bf16[128,4096]{1,0:T(8,128)(2,1)} %param.7) | copy-start | bytes 3145732
  2.8 41.5 %all-to-all-start.2 = ((bf16[128,32,128]{2,0,1:T(8,128)(2,1)}), bf16[128,32,128]{2,0,1:T(8,128)(2,1)S(1)}, u32[]{:S(2)}, u32[]{:S(2)}) async-start(bf16[128,32,128]{2,0,1:T(8,128)(2,1)} %bitcast.22), calls=%async_computation.2 | async-start | bytes 2097152 | tf_op jit(solution)/shard_map/all_to_all | solution.py:108
  45.5 33.7 %all-to-all-start = ((bf16[128,32,128]{2,0,1:T(8,128)(2,1)}), bf16[128,32,128]{2,0,1:T(8,128)(2,1)S(1)}, u32[]{:S(2)}, u32[]{:S(2)}) async-start(bf16[128,32,128]{2,0,1:T(8,128)(2,1)} %bitcast.16), calls=%async_computation | async-start | bytes 2097152 | tf_op jit(solution)/shard_map/all_to_all | solution.py:107
  79.2 40.4 %copy-start.16 = (s32[9]{0:T(128)S(1)}, s32[9]{0:T(128)}, u32[]{:S(2)}) copy-start(s32[9]{0:T(128)} %param.11) | copy-start | bytes 112
  79.2 35.5 %all-to-all-start.1 = ((bf16[128,32,128]{0,2,1:T(8,128)(2,1)}), bf16[128,32,128]{0,2,1:T(8,128)(2,1)S(1)}, u32[]{:S(2)}, u32[]{:S(2)}) async-start(bf16[128,32,128]{0,2,1:T(8,128)(2,1)} %bitcast.147), calls=%async_computation.1 | async-start | bytes 2097152 | tf_op jit(solution)/shard_map/all_to_all | solution.py:106
  114.7 33.4 %all-to-all-start.3 = ((bf16[128,32,128]{0,2,1:T(8,128)(2,1)}), bf16[128,32,128]{0,2,1:T(8,128)(2,1)}, u32[]{:S(2)}, u32[]{:S(2)}) async-start(bf16[128,32,128]{0,2,1:T(8,128)(2,1)} %bitcast.144), calls=%async_computation.3 | async-start | bytes 2097152 | tf_op jit(solution)/shard_map/all_to_all | solution.py:109
  153.7 9.1 %copy-start.3 = (s32[5120]{0:T(1024)}, s32[5120]{0:T(1024)S(1)}, u32[]{:S(2)}) copy-start(s32[5120]{0:T(1024)S(1)} %get-tuple-element.336) | copy-start | bytes 61444 | tf_op jit(solution)/shard_map/while
  153.7 9.1 %copy-start.17 = (s32[8]{0:T(128)}, s32[8]{0:T(128)S(1)}, u32[]{:S(2)}) copy-start(s32[8]{0:T(128)S(1)} %get-tuple-element.335) | copy-start | bytes 100 | tf_op jit(solution)/shard_map/while
  166.2 5.6 copy-start.12
  172.8 4.6 copy-start.6
  181.9 6.2 %copy-start.1 = (f32[1536,128]{1,0:T(8,128)S(1)}, f32[1536,128]{1,0:T(8,128)}, u32[]{:S(2)}) copy-start(f32[1536,128]{1,0:T(8,128)} %convolution_add_fusion.2) | copy-start | bytes 2359300 | tf_op jit(solution)/shard_map/while
  181.9 9.7 %copy-start.4 = (s32[5120]{0:T(1024)S(1)}, s32[5120]{0:T(1024)}, u32[]{:S(2)}) copy-start(s32[5120]{0:T(1024)} %copy-done.3) | copy-start | bytes 61444 | tf_op jit(solution)/shard_map/while
  181.9 9.7 %copy-start.18 = (s32[8]{0:T(128)S(1)}, s32[8]{0:T(128)}, u32[]{:S(2)}) copy-start(s32[8]{0:T(128)} %copy-done.17) | copy-start | bytes 100 | tf_op jit(solution)/shard_map/while
  191.6 9.1 %copy-start.3 = (s32[5120]{0:T(1024)}, s32[5120]{0:T(1024)S(1)}, u32[]{:S(2)}) copy-start(s32[5120]{0:T(1024)S(1)} %get-tuple-element.336) | copy-start | bytes 61444 | tf_op jit(solution)/shard_map/while
  191.6 9.1 %copy-start.17 = (s32[8]{0:T(128)}, s32[8]{0:T(128)S(1)}, u32[]{:S(2)}) copy-start(s32[8]{0:T(128)S(1)} %get-tuple-element.335) | copy-start | bytes 100 | tf_op jit(solution)/shard_map/while
  204.2 5.6 copy-start.12
  210.8 4.6 copy-start.6
  219.8 6.2 %copy-start.1 = (f32[1536,128]{1,0:T(8,128)S(1)}, f32[1536,128]{1,0:T(8,128)}, u32[]{:S(2)}) copy-start(f32[1536,128]{1,0:T(8,128)} %convolution_add_fusion.2) | copy-start | bytes 2359300 | tf_op jit(solution)/shard_map/while
  219.8 9.7 %copy-start.4 = (s32[5120]{0:T(1024)S(1)}, s32[5120]{0:T(1024)}, u32[]{:S(2)}) copy-start(s32[5120]{0:T(1024)} %copy-done.3) | copy-start | bytes 61444 | tf_op jit(solution)/shard_map/while
  219.9 9.7 %copy-start.18 = (s32[8]{0:T(128)S(1)}, s32[8]{0:T(128)}, u32[]{:S(2)}) copy-start(s32[8]{0:T(128)} %copy-done.17) | copy-start | bytes 100 | tf_op jit(solution)/shard_map/while
  229.6 9.1 %copy-start.3 = (s32[5120]{0:T(1024)}, s32[5120]{0:T(1024)S(1)}, u32[]{:S(2)}) copy-start(s32[5120]{0:T(1024)S(1)} %get-tuple-element.336) | copy-start | bytes 61444 | tf_op jit(solution)/shard_map/while
  229.6 9.1 %copy-start.17 = (s32[8]{0:T(128)}, s32[8]{0:T(128)S(1)}, u32[]{:S(2)}) copy-start(s32[8]{0:T(128)S(1)} %get-tuple-element.335) | copy-start | bytes 100 | tf_op jit(solution)/shard_map/while
  242.1 5.6 copy-start.12
  248.7 4.6 copy-start.6
  257.8 6.2 %copy-start.1 = (f32[1536,128]{1,0:T(8,128)S(1)}, f32[1536,128]{1,0:T(8,128)}, u32[]{:S(2)}) copy-start(f32[1536,128]{1,0:T(8,128)} %convolution_add_fusion.2) | copy-start | bytes 2359300 | tf_op jit(solution)/shard_map/while
  257.8 9.7 %copy-start.4 = (s32[5120]{0:T(1024)S(1)}, s32[5120]{0:T(1024)}, u32[]{:S(2)}) copy-start(s32[5120]{0:T(1024)} %copy-done.3) | copy-start | bytes 61444 | tf_op jit(solution)/shard_map/while
  257.8 9.7 %copy-start.18 = (s32[8]{0:T(128)S(1)}, s32[8]{0:T(128)}, u32[]{:S(2)}) copy-start(s32[8]{0:T(128)} %copy-done.17) | copy-start | bytes 100 | tf_op jit(solution)/shard_map/while
  267.5 9.1 %copy-start.3 = (s32[5120]{0:T(1024)}, s32[5120]{0:T(1024)S(1)}, u32[]{:S(2)}) copy-start(s32[5120]{0:T(1024)S(1)} %get-tuple-element.336) | copy-start | bytes 61444 | tf_op jit(solution)/shard_map/while
  267.5 9.1 %copy-start.17 = (s32[8]{0:T(128)}, s32[8]{0:T(128)S(1)}, u32[]{:S(2)}) copy-start(s32[8]{0:T(128)S(1)} %get-tuple-element.335) | copy-start | bytes 100 | tf_op jit(solution)/shard_map/while
  280.0 5.6 copy-start.12
  286.6 4.6 copy-start.6
  295.7 6.2 %copy-start.1 = (f32[1536,128]{1,0:T(8,128)S(1)}, f32[1536,128]{1,0:T(8,128)}, u32[]{:S(2)}) copy-start(f32[1536,128]{1,0:T(8,128)} %convolution_add_fusion.2) | copy-start | bytes 2359300 | tf_op jit(solution)/shard_map/while
  295.7 9.7 %copy-start.4 = (s32[5120]{0:T(1024)S(1)}, s32[5120]{0:T(1024)}, u32[]{:S(2)}) copy-start(s32[5120]{0:T(1024)} %copy-done.3) | copy-start | bytes 61444 | tf_op jit(solution)/shard_map/while
  295.7 9.7 %copy-start.18 = (s32[8]{0:T(128)S(1)}, s32[8]{0:T(128)}, u32[]{:S(2)}) copy-start(s32[8]{0:T(128)} %copy-done.17) | copy-start | bytes 100 | tf_op jit(solution)/shard_map/while
  305.4 9.1 %copy-start.3 = (s32[5120]{0:T(1024)}, s32[5120]{0:T(1024)S(1)}, u32[]{:S(2)}) copy-start(s32[5120]{0:T(1024)S(1)} %get-tuple-element.336) | copy-start | bytes 61444 | tf_op jit(solution)/shard_map/while
  305.4 9.1 %copy-start.17 = (s32[8]{0:T(128)}, s32[8]{0:T(128)S(1)}, u32[]{:S(2)}) copy-start(s32[8]{0:T(128)S(1)} %get-tuple-element.335) | copy-start | bytes 100 | tf_op jit(solution)/shard_map/while
  317.9 5.6 copy-start.12
  324.5 4.6 copy-start.6
  333.6 6.2 %copy-start.1 = (f32[1536,128]{1,0:T(8,128)S(1)}, f32[1536,128]{1,0:T(8,128)}, u32[]{:S(2)}) copy-start(f32[1536,128]{1,0:T(8,128)} %convolution_add_fusion.2) | copy-start | bytes 2359300 | tf_op jit(solution)/shard_map/while
  333.6 9.7 %copy-start.4 = (s32[5120]{0:T(1024)S(1)}, s32[5120]{0:T(1024)}, u32[]{:S(2)}) copy-start(s32[5120]{0:T(1024)} %copy-done.3) | copy-start | bytes 61444 | tf_op jit(solution)/shard_map/while
  333.6 9.7 %copy-start.18 = (s32[8]{0:T(128)S(1)}, s32[8]{0:T(128)}, u32[]{:S(2)}) copy-start(s32[8]{0:T(128)} %copy-done.17) | copy-start | bytes 100 | tf_op jit(solution)/shard_map/while
  343.4 9.1 %copy-start.3 = (s32[5120]{0:T(1024)}, s32[5120]{0:T(1024)S(1)}, u32[]{:S(2)}) copy-start(s32[5120]{0:T(1024)S(1)} %get-tuple-element.336) | copy-start | bytes 61444 | tf_op jit(solution)/shard_map/while
  343.4 9.1 %copy-start.17 = (s32[8]{0:T(128)}, s32[8]{0:T(128)S(1)}, u32[]{:S(2)}) copy-start(s32[8]{0:T(128)S(1)} %get-tuple-element.335) | copy-start | bytes 100 | tf_op jit(solution)/shard_map/while
  355.9 5.5 copy-start.12
  362.5 4.6 copy-start.6
  371.5 6.2 %copy-start.1 = (f32[1536,128]{1,0:T(8,128)S(1)}, f32[1536,128]{1,0:T(8,128)}, u32[]{:S(2)}) copy-start(f32[1536,128]{1,0:T(8,128)} %convolution_add_fusion.2) | copy-start | bytes 2359300 | tf_op jit(solution)/shard_map/while
  371.6 9.7 %copy-start.4 = (s32[5120]{0:T(1024)S(1)}, s32[5120]{0:T(1024)}, u32[]{:S(2)}) copy-start(s32[5120]{0:T(1024)} %copy-done.3) | copy-start | bytes 61444 | tf_op jit(solution)/shard_map/while
  371.6 9.7 %copy-start.18 = (s32[8]{0:T(128)S(1)}, s32[8]{0:T(128)}, u32[]{:S(2)}) copy-start(s32[8]{0:T(128)} %copy-done.17) | copy-start | bytes 100 | tf_op jit(solution)/shard_map/while
  381.3 9.1 %copy-start.3 = (s32[5120]{0:T(1024)}, s32[5120]{0:T(1024)S(1)}, u32[]{:S(2)}) copy-start(s32[5120]{0:T(1024)S(1)} %get-tuple-element.336) | copy-start | bytes 61444 | tf_op jit(solution)/shard_map/while
  381.3 9.1 %copy-start.17 = (s32[8]{0:T(128)}, s32[8]{0:T(128)S(1)}, u32[]{:S(2)}) copy-start(s32[8]{0:T(128)S(1)} %get-tuple-element.335) | copy-start | bytes 100 | tf_op jit(solution)/shard_map/while
  393.8 5.6 copy-start.12
  409.5 6.2 %copy-start.1 = (f32[1536,128]{1,0:T(8,128)S(1)}, f32[1536,128]{1,0:T(8,128)}, u32[]{:S(2)}) copy-start(f32[1536,128]{1,0:T(8,128)} %convolution_add_fusion.2) | copy-start | bytes 2359300 | tf_op jit(solution)/shard_map/while
  409.5 9.7 %copy-start.4 = (s32[5120]{0:T(1024)S(1)}, s32[5120]{0:T(1024)}, u32[]{:S(2)}) copy-start(s32[5120]{0:T(1024)} %copy-done.3) | copy-start | bytes 61444 | tf_op jit(solution)/shard_map/while
  409.5 9.7 %copy-start.18 = (s32[8]{0:T(128)S(1)}, s32[8]{0:T(128)}, u32[]{:S(2)}) copy-start(s32[8]{0:T(128)} %copy-done.17) | copy-start | bytes 100 | tf_op jit(solution)/shard_map/while
  419.2 9.1 %copy-start.3 = (s32[5120]{0:T(1024)}, s32[5120]{0:T(1024)S(1)}, u32[]{:S(2)}) copy-start(s32[5120]{0:T(1024)S(1)} %get-tuple-element.336) | copy-start | bytes 61444 | tf_op jit(solution)/shard_map/while
  419.2 9.1 %copy-start.17 = (s32[8]{0:T(128)}, s32[8]{0:T(128)S(1)}, u32[]{:S(2)}) copy-start(s32[8]{0:T(128)S(1)} %get-tuple-element.335) | copy-start | bytes 100 | tf_op jit(solution)/shard_map/while
  431.7 5.5 copy-start.12
  447.4 5.7 copy-start.1
  447.4 8.6 %copy-start.4 = (s32[5120]{0:T(1024)S(1)}, s32[5120]{0:T(1024)}, u32[]{:S(2)}) copy-start(s32[5120]{0:T(1024)} %copy-done.3) | copy-start | bytes 61444 | tf_op jit(solution)/shard_map/while
  447.4 8.6 %copy-start.18 = (s32[8]{0:T(128)S(1)}, s32[8]{0:T(128)}, u32[]{:S(2)}) copy-start(s32[8]{0:T(128)} %copy-done.17) | copy-start | bytes 100 | tf_op jit(solution)/shard_map/while
  490.0 33.7 %all-to-all-start.4 = ((bf16[32,128,128]{2,1,0:T(8,128)(2,1)}), bf16[32,128,128]{2,1,0:T(8,128)(2,1)S(1)}, u32[]{:S(2)}, u32[]{:S(2)}) async-start(bf16[32,128,128]{2,1,0:T(8,128)(2,1)} %bitcast.153), calls=%async_computation.4 | async-start | bytes 2097152 | tf_op jit(solution)/shard_map/all_to_all | solution.py:122
  523.7 33.6 %all-to-all-start.6 = ((bf16[32,128,128]{2,1,0:T(8,128)(2,1)}), bf16[32,128,128]{2,1,0:T(8,128)(2,1)S(1)}, u32[]{:S(2)}, u32[]{:S(2)}) async-start(bf16[32,128,128]{2,1,0:T(8,128)(2,1)} %bitcast.146), calls=%async_computation.6 | async-start | bytes 2097152 | tf_op jit(solution)/shard_map/all_to_all | solution.py:138
  557.3 34.1 %all-to-all-start.7 = ((bf16[32,128,128]{2,1,0:T(8,128)(2,1)}), bf16[32,128,128]{2,1,0:T(8,128)(2,1)}, u32[]{:S(2)}, u32[]{:S(2)}) async-start(bf16[32,128,128]{2,1,0:T(8,128)(2,1)} %bitcast.145), calls=%async_computation.7 | async-start | bytes 2097152 | tf_op jit(solution)/shard_map/all_to_all | solution.py:141
  (75 other events, 301.8 us)
where the time goes:
time: 599 us; the launch traced here: 594 us
  waiting for transfers between devices  183 us (31%)
  matrix products  143 us (24%)
  local copies, waits for them, and re-layouts  118 us (20%)
  loops' own time  43.5 us (7%)
  starting transfers between devices  42.9 us (7%)
  blocking collectives  34 us (6%)
  other arithmetic  28.7 us (5%)
    another operation x1, loops' own time, head_pass(): (k_acc, v_acc), (attended, q_grad) = lax.scan(step, (empty, empty), starts)  43.5 us
    dot_general x8, matrix products, block_pass(): jnp.einsum('hqk,qhd->kd', weights, o_grad, preferred_element_type=jnp.flo...  36.1 us
    all_to_all x1, blocking collectives, body(): lax.all_to_all(q_grad.reshape(length, heads_here * width), 'context', spl...  34 us
    dot_general x8, matrix products, block_pass(): jnp.einsum('hqk,kd->qhd', weights, v_window, preferred_element_type=jnp.f...  30.7 us
    all_to_all x1, waiting for transfers between devices, body(): lax.all_to_all(v_slots, 'context', split_axis=1, concat_axis=0, tiled=True)  28.9 us
    dynamic_update_slice x8, local copies, waits for them, and re-layouts, step(): lax.dynamic_update_slice_in_dim(v_acc, lax.dynamic_slice_in_dim(v_acc, st...  27.4 us
    dynamic_update_slice x8, local copies, waits for them, and re-layouts, step(): lax.dynamic_update_slice_in_dim(k_acc, lax.dynamic_slice_in_dim(k_acc, st...  27.3 us
    all_to_all x1, waiting for transfers between devices, body(): lax.all_to_all(k_slots, 'context', split_axis=1, concat_axis=0, tiled=True)  27.1 us
  transfers between devices with their start and end apart: 7, of which 7 were waited for; matrix products, arithmetic and copies ran while one was open for 3% of the time, Pallas kernels for 0%

commit v1 on v0

v1 whole, which is shorter than its diff:
```python
import functools

import jax
import jax.numpy as jnp
from jax import lax
from jax.experimental import pallas as pl
from jax.experimental.pallas import tpu as pltpu
from jax.sharding import PartitionSpec as P

BF = jnp.bfloat16
F32 = jnp.float32
MESH = pl.DeviceIdType.MESH
MASKED = -1e30
SCALE = 128 ** -0.5
SCALE2 = SCALE * 1.4426950408889634
SLOTS = 3
CHIPS = 16
BACK = 4


def nt(a, b):
    return lax.dot_general(a, b, (((1,), (1,)), ((), ())), preferred_element_type=F32)


def nn(a, b):
    return jnp.dot(a, b, preferred_element_type=F32)


def in_doc(pos0, bounds):
    pos = lax.broadcasted_iota(jnp.int32, (128, 128), 0) + pos0
    lane = lax.broadcasted_iota(jnp.int32, (128, 128), 1)
    hit = jnp.zeros((128, 128), F32)
    for t in range(8):
        inside = (pos >= bounds[t]) & (pos < bounds[t + 1]) & (lane == t)
        hit = jnp.where(inside, 1.0, hit)
    return hit, lane < 8


def prep_masks(q0, bounds, ka, qa):
    for a in range(2):
        hit, _ = in_doc(q0 + a * 128, bounds)
        qa[a, 0:128, :] = hit.astype(BF)
        qa[a, 128:256, :] = hit.astype(BF)
    for j in range(10):
        hit, lanes = in_doc(q0 - 1024 + j * 128, bounds)
        ka[j * 128 : (j + 1) * 128, :] = jnp.where(lanes, (1.0 - hit) * MASKED, 0.0).astype(BF)


def prep_transposed(g, kv, kt, vt):
    for j in range(10):
        r = slice(j * 128, (j + 1) * 128)
        kt[g, :, r] = kv[g, 0, r, :].T
        vt[g, 0:128, r] = kv[g, 1, r, :].T


def pair(ref, a, h):
    return jnp.concatenate(
        [ref[a, :, h * 128 : h * 128 + 128], ref[a, :, h * 128 + 128 : h * 128 + 256]], axis=0
    )


def scores(g, i, qv, kv, ka, qa, s):
    a, hp = i // 4, i % 4
    q = jnp.concatenate([pair(qv, a, g * 8 + hp * 2), qa[a]], axis=1)
    m = jnp.full((8, 256), -3e38, F32)
    for kc in range(9):
        r = slice((a + kc) * 128, (a + kc + 1) * 128)
        sc = nt(jnp.concatenate([kv[g, 0, r, :], ka[r, :]], axis=1), q)
        if kc == 8:
            key = lax.broadcasted_iota(jnp.int32, (128, 256), 0)
            query = lax.broadcasted_iota(jnp.int32, (128, 256), 1) % 128
            sc = jnp.where(key <= query, sc, MASKED)
        s[i % SLOTS, kc * 128 : (kc + 1) * 128, :] = sc
        m = jnp.maximum(m, jnp.max(sc.reshape(16, 8, 256), axis=0))
    return jnp.max(m, axis=0, keepdims=True) * SCALE2


def exps(i, m, s, e):
    for kc in range(9):
        r = slice(kc * 128, (kc + 1) * 128)
        e[i, r, :] = jnp.exp2(s[i % SLOTS, r, :] * SCALE2 - m).astype(BF)


def attend(g, i, gv, vt, e, gs, dd, ov):
    a, hp = i // 4, i % 4
    h = g * 8 + hp * 2
    ot = nn(vt[g, :, a * 128 : a * 128 + 1152], e[i])
    o = ot[0:128].T
    linv = 1.0 / ot[128:136].T[:, 0:1]
    o = o * linv
    gp = (pair(gv, a, h).astype(F32) * linv).astype(BF)
    gs[i] = gp
    d = gp.astype(F32) * o
    dd[i] = jnp.broadcast_to(jnp.sum(d.T, axis=0, keepdims=True), (8, 256))
    ob = o.astype(BF)
    ov[a, :, h * 128 : h * 128 + 128] = ob[0:128]
    ov[a, :, h * 128 + 128 : h * 128 + 256] = ob[128:256]


def forward(g, qv, gv, kv, ka, qa, vt, s, e, gs, dd, ov):
    m = {}
    for t in range(10):
        if t < 8:
            m[t] = scores(g, t, qv, kv, ka, qa, s)
        if 1 <= t < 9:
            exps(t - 1, m[t - 1], s, e)
        if 2 <= t:
            attend(g, t - 2, gv, vt, e, gs, dd, ov)


def key_grads(g, kc, qv, kv, e, gs, dd, part):
    r = slice(kc * 128, (kc + 1) * 128)
    values = kv[g, 1, r, :]
    dk = jnp.zeros((128, 128), F32)
    dv = jnp.zeros((128, 128), F32)
    for a in range(2):
        if not 0 <= kc - a <= 8:
            continue
        rr = slice((kc - a) * 128, (kc - a + 1) * 128)
        for hp in range(4):
            i = a * 4 + hp
            dp = nt(values, gs[i])
            ei = e[i, rr, :]
            ds = ei * (dp - dd[i, 0:1, :]).astype(BF)
            e[i, rr, :] = ds
            dv = dv + nn(ei, gs[i])
            dk = dk + nn(ds, pair(qv, a, g * 8 + hp * 2))
    part[g, kc, 0] = (dk * SCALE).astype(BF)
    part[g, kc, 1] = dv.astype(BF)


def query_grads(g, i, kt, e, dqv):
    a, hp = i // 4, i % 4
    h = g * 8 + hp * 2
    dq = (nn(kt[g, :, a * 128 : a * 128 + 1152], e[i]) * SCALE).T.astype(BF)
    dqv[a, :, h * 128 : h * 128 + 128] = dq[0:128]
    dqv[a, :, h * 128 + 128 : h * 128 + 256] = dq[128:256]


def kernel(
    bounds, q_in, k_in, v_in, g_in,
    o_out, dq_out, dk_out, dv_out,
    qv, gv, kv, ka, qa, kt, vt, s, e, gs, dd, ov, dqv, part, got,
    own_sem, kv_own_sem, row_send, row_recv, kv_send, kv_recv, part_send, part_recv,
    out_own_sem, out_send, out_recv,
):
    dp = lax.axis_index("dp")
    c = lax.axis_index("context")
    chip, core = c // 2, c % 2
    other = 1 - core
    partner = chip * 2 + other

    def at(step, p):
        return lax.rem(chip + step + CHIPS, CHIPS) * 2 + p

    def cols(p, g, width):
        return pl.ds(pl.multiple_of(p * (2 * width) + g * width, width), width)

    def remote(src, dst, send, recv, to):
        return pltpu.make_async_remote_copy(
            src_ref=src, dst_ref=dst, send_sem=send, recv_sem=recv,
            device_id=(dp, to), device_id_type=MESH,
        )

    barrier = pltpu.get_barrier_semaphore()
    peers = [partner]
    for j in range(1, BACK + 1):
        for p in range(2):
            peers += [at(j, p), at(-j, p)]
    for peer in peers:
        pl.semaphore_signal(barrier, inc=1, device_id=(dp, peer), device_id_type=MESH)

    own = []
    for g in range(2):
        for n, (src, dst) in enumerate(((q_in, qv), (g_in, gv))):
            own.append(pltpu.make_async_copy(
                src.at[:, cols(core, g, 1024)], dst.at[core, :, g * 1024 : (g + 1) * 1024],
                own_sem.at[g, n]))
        for n, src in enumerate((k_in, v_in)):
            own.append(pltpu.make_async_copy(
                src.at[:, cols(core, g, 128)],
                kv.at[g, n, pl.ds(pl.multiple_of(1024 + core * 128, 128), 128)],
                kv_own_sem.at[g, n]))
    for copy in own:
        copy.start()
    pl.semaphore_wait(barrier, len(peers))

    def row_copy(g, n, src, dst):
        return remote(src.at[:, cols(other, g, 1024)], dst.at[core, :, g * 1024 : (g + 1) * 1024],
                      row_send.at[g, n], row_recv.at[g, n], partner)

    def kv_copy(g, n, j, p):
        src = (k_in, v_in)[n]
        chunk = (BACK - j) * 2 + core
        return remote(src.at[:, cols(p, g, 128)],
                      kv.at[g, n, pl.ds(pl.multiple_of(chunk * 128, 128), 128)],
                      kv_send.at[g, n, j, p], kv_recv.at[g, n, j, core], at(j, p))

    def kv_arrived(g, n, j, q):
        dst = kv.at[g, n, ((BACK - j) * 2 + q) * 128 : ((BACK - j) * 2 + q + 1) * 128]
        remote(dst, dst, kv_send.at[g, n, j, q], kv_recv.at[g, n, j, q], partner).wait_recv()

    sends = []
    for g in range(2):
        for n, (src, dst) in enumerate(((q_in, qv), (g_in, gv))):
            sends.append(row_copy(g, n, src, dst))
        for n in range(2):
            sends.append(kv_copy(g, n, 0, other))
            for j in (1, 3, 2, 4):
                for p in range(2):
                    sends.append(kv_copy(g, n, j, p))
    for copy in sends:
        copy.start()

    prep_masks(c // 2 * 256, bounds, ka, qa)
    vt[0, 128:144, :] = jnp.ones((16, 1280), BF)
    vt[1, 128:144, :] = jnp.ones((16, 1280), BF)

    def part_copy(g, kc):
        j, q = BACK - kc // 2, kc % 2
        return remote(part.at[g, kc], got.at[g, j, core], part_send.at[g, kc],
                      part_recv.at[g, j, core], at(-j, q))

    def out_copies(g, n, src, dst):
        here = pltpu.make_async_copy(
            src.at[core, :, g * 1024 : (g + 1) * 1024], dst.at[:, cols(core, g, 1024)],
            out_own_sem.at[g, n])
        there = remote(src.at[other, :, g * 1024 : (g + 1) * 1024], dst.at[:, cols(core, g, 1024)],
                       out_send.at[g, n], out_recv.at[g, n], partner)
        return here, there

    outs = []
    for g in range(2):
        for copy in own[g * 4 : g * 4 + 4]:
            copy.wait()
        for n, (src, dst) in enumerate(((q_in, qv), (g_in, gv))):
            row = dst.at[other, :, g * 1024 : (g + 1) * 1024]
            remote(row, row, row_send.at[g, n], row_recv.at[g, n], partner).wait_recv()
        for n in range(2):
            dst = kv.at[g, n, pl.ds(pl.multiple_of(1024 + other * 128, 128), 128)]
            remote(dst, dst, kv_send.at[g, n, 0, other], kv_recv.at[g, n, 0, other], partner).wait_recv()
            for j in range(1, BACK + 1):
                for q in range(2):
                    kv_arrived(g, n, j, q)
        prep_transposed(g, kv, kt, vt)
        forward(g, qv, gv, kv, ka, qa, vt, s, e, gs, dd, ov)
        outs += out_copies(g, 0, ov, o_out)
        outs[-1].start()
        outs[-2].start()
        for kc in range(8):
            key_grads(g, kc, qv, kv, e, gs, dd, part)
            part_copy(g, kc).start()
        key_grads(g, 8, qv, kv, e, gs, dd, part)
        key_grads(g, 9, qv, kv, e, gs, dd, part)
        remote(part.at[g, 8 + other], got.at[g, 0, core], part_send.at[g, 8],
               part_recv.at[g, 0, core], partner).start()
        for i in range(8):
            query_grads(g, i, kt, e, dqv)
        outs += out_copies(g, 1, dqv, dq_out)
        outs[-1].start()
        outs[-2].start()

    for g in range(2):
        for j in range(1, BACK + 1):
            for p in range(2):
                dst = got.at[g, j, p]
                remote(dst, dst, part_send.at[g, j], part_recv.at[g, j, p], partner).wait_recv()
        dst = got.at[g, 0, other]
        remote(dst, dst, part_send.at[g, 8], part_recv.at[g, 0, other], partner).wait_recv()
        got[g, 0, core] = part[g, 8 + core]
        for p in range(2):
            for n, out in enumerate((dk_out, dv_out)):
                total = got[g, 0, p, n].astype(F32)
                for j in range(1, BACK + 1):
                    total = total + got[g, j, p, n].astype(F32)
                out[:, (2 * p + g) * 128 : (2 * p + g + 1) * 128] = total.astype(BF)

    for copy in sends:
        copy.wait_send()
    for g in range(2):
        for kc in range(8):
            part_copy(g, kc).wait_send()
        remote(part.at[g, 8 + other], got.at[g, 0, core], part_send.at[g, 8],
               part_recv.at[g, 0, core], partner).wait_send()
        for n, (src, dst) in enumerate(((ov, o_out), (dqv, dq_out))):
            here, there = out_copies(g, n, src, dst)
            here.wait()
            there.wait_send()
            arrived = dst.at[:, cols(other, g, 1024)]
            remote(arrived, arrived, out_send.at[g, n], out_recv.at[g, n], partner).wait_recv()


def body(query_rows, key_rows, value_rows, grad_out, doc_bounds):
    hbm = pl.BlockSpec(memory_space=pl.ANY)
    vmem = pl.BlockSpec(memory_space=pltpu.VMEM)
    rows = jax.ShapeDtypeStruct((128, 4096), BF)
    small = jax.ShapeDtypeStruct((128, 512), BF)
    dma = pltpu.SemaphoreType.DMA
    return pl.pallas_call(
        kernel,
        out_shape=(rows, rows, small, small),
        in_specs=[pl.BlockSpec(memory_space=pltpu.SMEM), hbm, hbm, hbm, hbm],
        out_specs=(hbm, hbm, vmem, vmem),
        scratch_shapes=[
            pltpu.VMEM((2, 128, 2048), BF),
            pltpu.VMEM((2, 128, 2048), BF),
            pltpu.VMEM((2, 2, 1280, 128), BF),
            pltpu.VMEM((1280, 128), BF),
            pltpu.VMEM((2, 256, 128), BF),
            pltpu.VMEM((2, 128, 1280), BF),
            pltpu.VMEM((2, 144, 1280), BF),
            pltpu.VMEM((SLOTS, 1152, 256), F32),
            pltpu.VMEM((8, 1152, 256), BF),
            pltpu.VMEM((8, 256, 128), BF),
            pltpu.VMEM((8, 8, 256), F32),
            pltpu.VMEM((2, 128, 2048), BF),
            pltpu.VMEM((2, 128, 2048), BF),
            pltpu.VMEM((2, 10, 2, 128, 128), BF),
            pltpu.VMEM((2, BACK + 1, 2, 2, 128, 128), BF),
            dma((2, 2)), dma((2, 2)), dma((2, 2)), dma((2, 2)),
            dma((2, 2, BACK + 1, 2)), dma((2, 2, BACK + 1, 2)),
            dma((2, 9)), dma((2, BACK + 1, 2)),
            dma((2, 2)), dma((2, 2)), dma((2, 2)),
        ],
        compiler_params=pltpu.CompilerParams(
            collective_id=0, has_side_effects=True, vmem_limit_bytes=56 << 20
        ),
        name="packed_attention",
    )(doc_bounds, query_rows, key_rows, value_rows, grad_out)


def solution(mesh):
    rows = P(("dp", "context"), None)
    return jax.shard_map(
        body,
        mesh=mesh,
        in_specs=(rows, rows, rows, rows, P("dp")),
        out_specs=(rows, rows, rows, rows),
        check_vma=False,
    )
```

time: 599 us -> 70.3 us (0.12)
  waiting for transfers between devices: 183 us -> 0 us
  matrix products: 143 us -> 0 us
  local copies, waits for them, and re-layouts: 118 us -> 5.01 us
  Pallas kernels: 0 us -> 64.4 us
  loops' own time: 43.5 us -> 0 us
  starting transfers between devices: 42.9 us -> 0 us
  blocking collectives: 34 us -> 0 us
  other arithmetic: 28.7 us -> 0 us
    all_to_all x7 -> x0, waiting for transfers between devices: 183 us -> none  [the longest x1 28.9 us: body(): lax.all_to_all(v_slots, 'context', split_axis=1, concat_axis=0, tiled=True)]
    dot_general x48 -> x0, matrix products: 143 us -> none  [the longest x8 36.1 us: block_pass(): jnp.einsum('hqk,qhd->kd', weights, o_grad, preferred_element_type=jnp.flo...]
    dynamic_update_slice x40 -> x0, local copies, waits for them, and re-layouts: 69.6 us -> none  [the longest x8 27.4 us: step(): lax.dynamic_update_slice_in_dim(v_acc, lax.dynamic_slice_in_dim(v_acc, st...]
    pallas_call x0 -> x1, Pallas kernels: none -> 64.4 us  [body(): pl.pallas_call(kernel, out_shape=(rows, rows, small, small), in_specs=[pl...]
    another operation x1 -> x0, loops' own time: 43.5 us -> none  [head_pass(): (k_acc, v_acc), (attended, q_grad) = lax.scan(step, (empty, empty), starts)]
    all_to_all x7 -> x0, starting transfers between devices: 42.9 us -> none  [the longest x1 12.6 us: body(): lax.all_to_all(v_slots, 'context', split_axis=1, concat_axis=0, tiled=True)]
    all_to_all x1 -> x0, blocking collectives: 34 us -> none  [body(): lax.all_to_all(q_grad.reshape(length, heads_here * width), 'context', spl...]
    dynamic_slice x40 -> x0, local copies, waits for them, and re-layouts: 18.6 us -> none  [the longest x16 8.45 us: step(): g_block = lax.dynamic_slice_in_dim(g_heads, start, QBLOCK, 0)]
  transfers between devices with their start and end apart: 7 -> 0, of which waited for: 7 -> 0; matrix products, arithmetic and copies ran while one was open for 3% -> 0% of each run, Pallas kernels for 0% -> 0%
where the time goes in v1:
time: 70.3 us; the launch traced here: 70.1 us
  Pallas kernels  64.4 us (92%)
  local copies, waits for them, and re-layouts  5.01 us (7%)
    pallas_call x1, Pallas kernels, body(): pl.pallas_call(kernel, out_shape=(rows, rows, small, small), in_specs=[pl...  64.4 us
    unnamed x10, local copies, waits for them, and re-layouts  5.01 us

profile of v1, /device:TPU:1, one launch (start us, length us, event | category | flops | bytes accessed | tf_op | source)
XLA Modules:
  0.0 70.1 jit_solution(3709087761096265453)
XLA Ops:
  0.6 64.4 %packed_attention.1 = (bf16[128,4096]{1,0:T(8,128)(2,1)}, bf16[128,4096]{1,0:T(8,128)(2,1)}, bf16[128,512]{1,0:T(8,128)(2,1)}, bf16[128,512]{1,0:T(8,128)(2,1)}) custom-call(s32[9]{0:T(128)} %bounds.1, bf16[128,4096]{1,0:T(8,128)(2,1)} %q_in.1, bf16[128,512]{1,0:T(8,128)(2,1)} %k_in.1, bf16[128,512]{1,0:T(8,128)(2,1)} %v_in.1, bf16[128,4096]{1,0:T(8,128)(2,1)} %g_in.1), custom_call_target="tpu_custom_call" | custom-call | tf_op jit(solution)/shard_map/packed_attention/pallas_call | solution.py:299
  65.1 0.0 copy-start
  65.1 2.4 %copy.13 = bf16[128,4096]{1,0:T(8,128)(2,1)} copy(bf16[128,4096]{1,0:T(8,128)(2,1)} %get-tuple-element.8) | data formatting | bytes 2097152
  67.5 0.0 copy-done
  67.5 0.0 copy-start.2
  67.5 1.0 %copy.14 = bf16[128,4096]{1,0:T(8,128)(2,1)} copy(bf16[128,4096]{1,0:T(8,128)(2,1)S(1)} %copy-done) | data formatting | bytes 2097152
  68.4 0.1 copy-done.2
  68.5 0.0 copy-start.1
  68.5 0.7 copy.15
  69.2 0.3 copy-done.1
  69.5 0.7 copy.16
Async XLA Ops:
  65.1 2.4 %copy-start = (bf16[128,4096]{1,0:T(8,128)(2,1)S(1)}, bf16[128,4096]{1,0:T(8,128)(2,1)}, u32[]{:S(2)}) copy-start(bf16[128,4096]{1,0:T(8,128)(2,1)} %get-tuple-element.9) | copy-start | bytes 3145732
  67.5 1.0 %copy-start.2 = (bf16[128,512]{1,0:T(8,128)(2,1)S(1)}, bf16[128,512]{1,0:T(8,128)(2,1)}, u32[]{:S(2)}) copy-start(bf16[128,512]{1,0:T(8,128)(2,1)} %get-tuple-element.10) | copy-start | bytes 393220
  68.5 1.0 %copy-start.1 = (bf16[128,512]{1,0:T(8,128)(2,1)S(1)}, bf16[128,512]{1,0:T(8,128)(2,1)}, u32[]{:S(2)}) copy-start(bf16[128,512]{1,0:T(8,128)(2,1)} %get-tuple-element.11) | copy-start | bytes 393220

commit v2 on v1

--- a/solution.py
+++ b/solution.py
@@ -15,6 +15,7 @@
 SCALE2 = SCALE * 1.4426950408889634
 SLOTS = 3
 CHIPS = 16
+PAIRS = (2, 0, 3, 1, 4)
 BACK = 4
 
 
@@ -46,11 +47,17 @@
         ka[j * 128 : (j + 1) * 128, :] = jnp.where(lanes, (1.0 - hit) * MASKED, 0.0).astype(BF)
 
 
-def prep_transposed(g, kv, kt, vt):
+def prep_transposed(g, n, kv, out):
     for j in range(10):
         r = slice(j * 128, (j + 1) * 128)
-        kt[g, :, r] = kv[g, 0, r, :].T
-        vt[g, 0:128, r] = kv[g, 1, r, :].T
+        out[g, 0:128, r] = kv[g, n, r, :].T
+
+
+def prep_rows(g, qv, qr):
+    for a in range(2):
+        for h in range(8):
+            r = a * 1024 + h * 128
+            qr[g, r : r + 128, :] = qv[a, :, (g * 8 + h) * 128 : (g * 8 + h + 1) * 128]
 
 
 def pair(ref, a, h):
@@ -59,80 +66,93 @@
     )
 
 
-def scores(g, i, qv, kv, ka, qa, s):
-    a, hp = i // 4, i % 4
-    q = jnp.concatenate([pair(qv, a, g * 8 + hp * 2), qa[a]], axis=1)
-    m = jnp.full((8, 256), -3e38, F32)
-    for kc in range(9):
-        r = slice((a + kc) * 128, (a + kc + 1) * 128)
-        sc = nt(jnp.concatenate([kv[g, 0, r, :], ka[r, :]], axis=1), q)
-        if kc == 8:
-            key = lax.broadcasted_iota(jnp.int32, (128, 256), 0)
-            query = lax.broadcasted_iota(jnp.int32, (128, 256), 1) % 128
-            sc = jnp.where(key <= query, sc, MASKED)
-        s[i % SLOTS, kc * 128 : (kc + 1) * 128, :] = sc
-        m = jnp.maximum(m, jnp.max(sc.reshape(16, 8, 256), axis=0))
+def window(i):
+    return slice(i // 4 * 128, i // 4 * 128 + 1152)
+
+
+def scores(g, i, qr, kv, ka, qa, s):
+    w = window(i)
+    q = jnp.concatenate([qr[g, i * 256 : (i + 1) * 256, :], qa[i // 4]], axis=1)
+    sc = nt(jnp.concatenate([kv[g, 0, w, :], ka[w, :]], axis=1), q)
+    key = lax.broadcasted_iota(jnp.int32, (128, 256), 0)
+    query = lax.broadcasted_iota(jnp.int32, (128, 256), 1) % 128
+    last = jnp.where(key <= query, sc[1024:], MASKED)
+    sc = jnp.concatenate([sc[:1024], last], axis=0)
+    s[i % SLOTS] = sc
+    m = jnp.max(sc.reshape(144, 8, 256), axis=0)
     return jnp.max(m, axis=0, keepdims=True) * SCALE2
 
 
 def exps(i, m, s, e):
-    for kc in range(9):
-        r = slice(kc * 128, (kc + 1) * 128)
-        e[i, r, :] = jnp.exp2(s[i % SLOTS, r, :] * SCALE2 - m).astype(BF)
-
-
-def attend(g, i, gv, vt, e, gs, dd, ov):
-    a, hp = i // 4, i % 4
-    h = g * 8 + hp * 2
-    ot = nn(vt[g, :, a * 128 : a * 128 + 1152], e[i])
+    e[window(i), i * 256 : (i + 1) * 256] = jnp.exp2(s[i % SLOTS] * SCALE2 - m).astype(BF)
+
+
+def attend(g, i, vt, e):
+    return nn(vt[g, :, window(i)], e[window(i), i * 256 : (i + 1) * 256])
+
+
+def finish(g, i, ot, gv, gs, ov):
+    a, h = i // 4, g * 8 + i % 4 * 2
     o = ot[0:128].T
     linv = 1.0 / ot[128:136].T[:, 0:1]
     o = o * linv
     gp = (pair(gv, a, h).astype(F32) * linv).astype(BF)
-    gs[i] = gp
-    d = gp.astype(F32) * o
-    dd[i] = jnp.broadcast_to(jnp.sum(d.T, axis=0, keepdims=True), (8, 256))
+    r = slice(i * 256, (i + 1) * 256)
+    gs[r, 0:128] = gp
+    gs[r, 128:256] = (-(gp.astype(F32) * o)).astype(BF)
     ob = o.astype(BF)
     ov[a, :, h * 128 : h * 128 + 128] = ob[0:128]
     ov[a, :, h * 128 + 128 : h * 128 + 256] = ob[128:256]
 
 
-def forward(g, qv, gv, kv, ka, qa, vt, s, e, gs, dd, ov):
-    m = {}
-    for t in range(10):
+def forward(g, qr, gv, kv, ka, qa, vt, s, e, gs, ov, beside):
+    m, ot = {}, {}
+    for t in range(11):
+        beside(t)
         if t < 8:
-            m[t] = scores(g, t, qv, kv, ka, qa, s)
+            m[t] = scores(g, t, qr, kv, ka, qa, s)
         if 1 <= t < 9:
             exps(t - 1, m[t - 1], s, e)
-        if 2 <= t:
-            attend(g, t - 2, gv, vt, e, gs, dd, ov)
-
-
-def key_grads(g, kc, qv, kv, e, gs, dd, part):
-    r = slice(kc * 128, (kc + 1) * 128)
-    values = kv[g, 1, r, :]
-    dk = jnp.zeros((128, 128), F32)
-    dv = jnp.zeros((128, 128), F32)
-    for a in range(2):
-        if not 0 <= kc - a <= 8:
-            continue
-        rr = slice((kc - a) * 128, (kc - a + 1) * 128)
-        for hp in range(4):
-            i = a * 4 + hp
-            dp = nt(values, gs[i])
-            ei = e[i, rr, :]
-            ds = ei * (dp - dd[i, 0:1, :]).astype(BF)
-            e[i, rr, :] = ds
-            dv = dv + nn(ei, gs[i])
-            dk = dk + nn(ds, pair(qv, a, g * 8 + hp * 2))
-    part[g, kc, 0] = (dk * SCALE).astype(BF)
-    part[g, kc, 1] = dv.astype(BF)
-
-
-def query_grads(g, i, kt, e, dqv):
-    a, hp = i // 4, i % 4
-    h = g * 8 + hp * 2
-    dq = (nn(kt[g, :, a * 128 : a * 128 + 1152], e[i]) * SCALE).T.astype(BF)
+        if 2 <= t < 10:
+            ot[t - 2] = attend(g, t - 2, vt, e)
+        if 3 <= t:
+            finish(g, t - 3, ot[t - 3], gv, gs, ov)
+
+
+def score_grads(g, pr, kv, e, gs, ds):
+    values = jnp.concatenate(
+        [kv[g, 1, pr * 256 : (pr + 1) * 256, :], jnp.ones((256, 128), BF)], axis=1
+    )
+    for i in range(8):
+        lo = 128 if i >= 4 and pr == 0 else 0
+        hi = 128 if i < 4 and pr == 4 else 256
+        r, c = slice(pr * 256 + lo, pr * 256 + hi), slice(i * 256, (i + 1) * 256)
+        dp = nt(values[lo:hi], gs[c, :])
+        ds[r, c] = e[r, c] * dp.astype(BF)
+
+
+def over_queries(pr, left, right):
+    r = pr * 256
+    if pr == 0:
+        return (nn(left[0:128, 0:1024], right(0, 1024)), nn(left[128:256, :], right(0, 2048)))
+    if pr == 4:
+        return (nn(left[r : r + 128, :], right(0, 2048)),
+                nn(left[r + 128 : r + 256, 1024:2048], right(1024, 2048)))
+    x = nn(left[r : r + 256, :], right(0, 2048))
+    return x[0:128], x[128:256]
+
+
+def key_grads(g, pr, qr, e, gs, ds, part):
+    dv = over_queries(pr, e, lambda x0, x1: gs[x0:x1, 0:128])
+    dk = over_queries(pr, ds, lambda x0, x1: qr[g, x0:x1, :])
+    for n in range(2):
+        part[g, pr * 2 + n, 0] = (dk[n] * SCALE).astype(BF)
+        part[g, pr * 2 + n, 1] = dv[n].astype(BF)
+
+
+def query_grads(g, i, kt, ds, dqv):
+    a, h = i // 4, g * 8 + i % 4 * 2
+    dq = (nn(kt[g, :, window(i)], ds[window(i), i * 256 : (i + 1) * 256]) * SCALE).T.astype(BF)
     dqv[a, :, h * 128 : h * 128 + 128] = dq[0:128]
     dqv[a, :, h * 128 + 128 : h * 128 + 256] = dq[128:256]
 
@@ -140,7 +160,7 @@
 def kernel(
     bounds, q_in, k_in, v_in, g_in,
     o_out, dq_out, dk_out, dv_out,
-    qv, gv, kv, ka, qa, kt, vt, s, e, gs, dd, ov, dqv, part, got,
+    qv, gv, kv, ka, qa, qr, kt, vt, s, e, ds, gs, ov, dqv, part, got,
     own_sem, kv_own_sem, row_send, row_recv, kv_send, kv_recv, part_send, part_recv,
     out_own_sem, out_send, out_recv,
 ):
@@ -200,26 +220,52 @@
         dst = kv.at[g, n, ((BACK - j) * 2 + q) * 128 : ((BACK - j) * 2 + q + 1) * 128]
         remote(dst, dst, kv_send.at[g, n, j, q], kv_recv.at[g, n, j, q], partner).wait_recv()
 
-    sends = []
+    sends = [[], []]
     for g in range(2):
         for n, (src, dst) in enumerate(((q_in, qv), (g_in, gv))):
-            sends.append(row_copy(g, n, src, dst))
+            sends[g].append(row_copy(g, n, src, dst))
         for n in range(2):
-            sends.append(kv_copy(g, n, 0, other))
-            for j in (1, 3, 2, 4):
+            sends[g].append(kv_copy(g, n, 0, other))
+            for j in (1, 3, 4):
                 for p in range(2):
-                    sends.append(kv_copy(g, n, j, p))
-    for copy in sends:
+                    sends[g].append(kv_copy(g, n, j, p))
+    for copy in sends[0]:
         copy.start()
 
     prep_masks(c // 2 * 256, bounds, ka, qa)
     vt[0, 128:144, :] = jnp.ones((16, 1280), BF)
     vt[1, 128:144, :] = jnp.ones((16, 1280), BF)
+    def relay(g, n, way):
+        src, dst, to = ((6, 4, 1), (3, 5, -1))[way]
+        return remote(kv.at[g, n, src * 128 : (src + 1) * 128], kv.at[g, n, dst * 128 : (dst + 1) * 128],
+                      kv_send.at[g, n, 2, way], kv_recv.at[g, n, 2, way], at(to, core))
+
+    def relay_when_here(g, n):
+        kv_arrived(g, n, 1, 0)
+        relay(g, n, 0).start()
+        kv_arrived(g, n, 3, 1)
+        relay(g, n, 1).start()
+
+    relay_when_here(0, 0)
+    relay_when_here(0, 1)
+    for copy in sends[1]:
+        copy.start()
 
     def part_copy(g, kc):
+        if kc in (4, 5):
+            to, way = ((-1, 0), (1, 1))[kc - 4]
+            return remote(part.at[g, kc], got.at[g, 2, way], part_send.at[g, kc],
+                          part_recv.at[g, 2, way], at(to, core))
         j, q = BACK - kc // 2, kc % 2
         return remote(part.at[g, kc], got.at[g, j, core], part_send.at[g, kc],
                       part_recv.at[g, j, core], at(-j, q))
+
+    def part_join(g, way):
+        kc = (6, 3)[way]
+        dst = got.at[g, 2, way]
+        remote(dst, dst, part_send.at[g, kc], part_recv.at[g, 2, way], partner).wait_recv()
+        part[g, kc] = (part[g, kc].astype(F32) + got[g, 2, way].astype(F32)).astype(BF)
+        part_copy(g, kc).start()
 
     def out_copies(g, n, src, dst):
         here = pltpu.make_async_copy(
@@ -236,32 +282,49 @@
         for n, (src, dst) in enumerate(((q_in, qv), (g_in, gv))):
             row = dst.at[other, :, g * 1024 : (g + 1) * 1024]
             remote(row, row, row_send.at[g, n], row_recv.at[g, n], partner).wait_recv()
+        prep_rows(g, qv, qr)
         for n in range(2):
             dst = kv.at[g, n, pl.ds(pl.multiple_of(1024 + other * 128, 128), 128)]
             remote(dst, dst, kv_send.at[g, n, 0, other], kv_recv.at[g, n, 0, other], partner).wait_recv()
             for j in range(1, BACK + 1):
                 for q in range(2):
-                    kv_arrived(g, n, j, q)
-        prep_transposed(g, kv, kt, vt)
-        forward(g, qv, gv, kv, ka, qa, vt, s, e, gs, dd, ov)
+                    if (j, q) not in ((1, 0), (3, 1)):
+                        kv_arrived(g, n, j, q)
+            prep_transposed(g, n, kv, (kt, vt)[n])
+
+        def beside(t):
+            if g == 0 and t in (8, 10):
+                relay_when_here(1, (t - 8) // 2)
+            if g == 1 and t in (3, 4):
+                part_join(0, t - 3)
+
+        forward(g, qr, gv, kv, ka, qa, vt, s, e, gs, ov, beside)
         outs += out_copies(g, 0, ov, o_out)
         outs[-1].start()
         outs[-2].start()
-        for kc in range(8):
-            key_grads(g, kc, qv, kv, e, gs, dd, part)
-            part_copy(g, kc).start()
-        key_grads(g, 8, qv, kv, e, gs, dd, part)
-        key_grads(g, 9, qv, kv, e, gs, dd, part)
-        remote(part.at[g, 8 + other], got.at[g, 0, core], part_send.at[g, 8],
-               part_recv.at[g, 0, core], partner).start()
+        for n in range(len(PAIRS) + 1):
+            if n < len(PAIRS):
+                score_grads(g, PAIRS[n], kv, e, gs, ds)
+            if n > 0:
+                pr = PAIRS[n - 1]
+                key_grads(g, pr, qr, e, gs, ds, part)
+                if pr < BACK:
+                    for kc in (2 * pr, 2 * pr + 1):
+                        if kc not in (3, 6):
+                            part_copy(g, kc).start()
+                else:
+                    remote(part.at[g, 8 + other], got.at[g, 0, core], part_send.at[g, 8],
+                           part_recv.at[g, 0, core], partner).start()
         for i in range(8):
-            query_grads(g, i, kt, e, dqv)
+            query_grads(g, i, kt, ds, dqv)
         outs += out_copies(g, 1, dqv, dq_out)
         outs[-1].start()
         outs[-2].start()
 
-    for g in range(2):
-        for j in range(1, BACK + 1):
+    part_join(1, 0)
+    part_join(1, 1)
+    for g in range(2):
+        for j in (1, 3, 4):
             for p in range(2):
                 dst = got.at[g, j, p]
                 remote(dst, dst, part_send.at[g, j], part_recv.at[g, j, p], partner).wait_recv()
@@ -271,12 +334,16 @@
         for p in range(2):
             for n, out in enumerate((dk_out, dv_out)):
                 total = got[g, 0, p, n].astype(F32)
-                for j in range(1, BACK + 1):
+                for j in (1, 3, 4):
                     total = total + got[g, j, p, n].astype(F32)
                 out[:, (2 * p + g) * 128 : (2 * p + g + 1) * 128] = total.astype(BF)
 
-    for copy in sends:
+    for copy in sends[0] + sends[1]:
         copy.wait_send()
+    for g in range(2):
+        for n in range(2):
+            for way in range(2):
+                relay(g, n, way).wait_send()
     for g in range(2):
         for kc in range(8):
             part_copy(g, kc).wait_send()
@@ -290,13 +357,32 @@
             remote(arrived, arrived, out_send.at[g, n], out_recv.at[g, n], partner).wait_recv()
 
 
+def hand_over(*refs):
+    src, dst, held, sems = refs[:4], refs[4:8], refs[8:12], refs[12]
+    way_in, way_out = [], []
+    for n in range(4):
+        pieces = 4 if n < 2 else 1
+        rows = src[n].shape[0] // pieces
+        for m in range(pieces):
+            r = pl.ds(m * rows, rows)
+            way_in.append(pltpu.make_async_copy(src[n].at[r], held[n].at[r], sems.at[0, n, m]))
+            way_out.append(pltpu.make_async_copy(held[n].at[r], dst[n].at[r], sems.at[1, n, m]))
+    for copy in way_in:
+        copy.start()
+    for here, there in zip(way_in, way_out):
+        here.wait()
+        there.start()
+    for copy in way_out:
+        copy.wait()
+
+
 def body(query_rows, key_rows, value_rows, grad_out, doc_bounds):
     hbm = pl.BlockSpec(memory_space=pl.ANY)
     vmem = pl.BlockSpec(memory_space=pltpu.VMEM)
     rows = jax.ShapeDtypeStruct((128, 4096), BF)
     small = jax.ShapeDtypeStruct((128, 512), BF)
     dma = pltpu.SemaphoreType.DMA
-    return pl.pallas_call(
+    results = pl.pallas_call(
         kernel,
         out_shape=(rows, rows, small, small),
         in_specs=[pl.BlockSpec(memory_space=pltpu.SMEM), hbm, hbm, hbm, hbm],
@@ -307,12 +393,13 @@
             pltpu.VMEM((2, 2, 1280, 128), BF),
             pltpu.VMEM((1280, 128), BF),
             pltpu.VMEM((2, 256, 128), BF),
+            pltpu.VMEM((2, 2048, 128), BF),
             pltpu.VMEM((2, 128, 1280), BF),
             pltpu.VMEM((2, 144, 1280), BF),
             pltpu.VMEM((SLOTS, 1152, 256), F32),
-            pltpu.VMEM((8, 1152, 256), BF),
-            pltpu.VMEM((8, 256, 128), BF),
-            pltpu.VMEM((8, 8, 256), F32),
+            pltpu.VMEM((1280, 2048), BF),
+            pltpu.VMEM((1280, 2048), BF),
+            pltpu.VMEM((2048, 256), BF),
             pltpu.VMEM((2, 128, 2048), BF),
             pltpu.VMEM((2, 128, 2048), BF),
             pltpu.VMEM((2, 10, 2, 128, 128), BF),
@@ -327,6 +414,14 @@
         ),
         name="packed_attention",
     )(doc_bounds, query_rows, key_rows, value_rows, grad_out)
+    return pl.pallas_call(
+        hand_over,
+        out_shape=(rows, rows, small, small),
+        in_specs=[hbm] * 4,
+        out_specs=[hbm] * 4,
+        scratch_shapes=[pltpu.VMEM(x.shape, BF) for x in (rows, rows, small, small)] + [dma((2, 4, 4))],
+        name="hand_over",
+    )(*results)
 
 
 def solution(mesh):

time: 70.3 us -> 60.1 us (0.85)
  the two profiles are of different devices: /device:TPU:1 before, /device:TPU:69 now
where the time goes in v2:
time: 60.1 us; the launch traced here: 59.9 us
  Pallas kernels  59.1 us (98%)
  between operations  0.8 us (1%)
    pallas_call x1, Pallas kernels, body(): pl.pallas_call(kernel, out_shape=(rows, rows, small, small), in_specs=[pl...  56.5 us
    pallas_call x1, Pallas kernels, body(): pl.pallas_call(hand_over, out_shape=(rows, rows, small, small), in_specs=...  2.62 us

profile of v2, /device:TPU:69, one launch (start us, length us, event | category | flops | bytes accessed | tf_op | source)
XLA Modules:
  0.0 59.9 jit_solution(14346390368597525373)
XLA Ops:
  0.6 56.5 %packed_attention.1 = (bf16[128,4096]{1,0:T(8,128)(2,1)}, bf16[128,4096]{1,0:T(8,128)(2,1)}, bf16[128,512]{1,0:T(8,128)(2,1)}, bf16[128,512]{1,0:T(8,128)(2,1)}) custom-call(s32[9]{0:T(128)} %bounds.1, bf16[128,4096]{1,0:T(8,128)(2,1)} %q_in.1, bf16[128,512]{1,0:T(8,128)(2,1)} %k_in.1, bf16[128,512]{1,0:T(8,128)(2,1)} %v_in.1, bf16[128,4096]{1,0:T(8,128)(2,1)} %g_in.1), custom_call_target="tpu_custom_call" | custom-call | tf_op jit(solution)/shard_map/packed_attention/pallas_call | solution.py:385
  57.2 2.6 %hand_over.1 = (bf16[128,4096]{1,0:T(8,128)(2,1)}, bf16[128,4096]{1,0:T(8,128)(2,1)}, bf16[128,512]{1,0:T(8,128)(2,1)}, bf16[128,512]{1,0:T(8,128)(2,1)}) custom-call(bf16[128,4096]{1,0:T(8,128)(2,1)} %get-tuple-element.8.refs_0_, bf16[128,4096]{1,0:T(8,128)(2,1)} %get-tuple-element.9.refs_1_, bf16[128,512]{1,0:T(8,128)(2,1)} %get-tuple-element.10.refs_2_, ...), custom_call_target="tpu_custom_call" | custom-call | tf_op jit(solution)/shard_map/hand_over/pallas_call | solution.py:417

commit v3 on v2

--- a/solution.py
+++ b/solution.py
@@ -240,14 +240,13 @@
         return remote(kv.at[g, n, src * 128 : (src + 1) * 128], kv.at[g, n, dst * 128 : (dst + 1) * 128],
                       kv_send.at[g, n, 2, way], kv_recv.at[g, n, 2, way], at(to, core))
 
-    def relay_when_here(g, n):
-        kv_arrived(g, n, 1, 0)
-        relay(g, n, 0).start()
-        kv_arrived(g, n, 3, 1)
-        relay(g, n, 1).start()
-
-    relay_when_here(0, 0)
-    relay_when_here(0, 1)
+    def relay_when_here(g, n, way):
+        kv_arrived(g, n, (1, 3)[way], way)
+        relay(g, n, way).start()
+
+    for n in range(2):
+        for way in range(2):
+            relay_when_here(0, n, way)
     for copy in sends[1]:
         copy.start()
 
@@ -293,8 +292,8 @@
             prep_transposed(g, n, kv, (kt, vt)[n])
 
         def beside(t):
-            if g == 0 and t in (8, 10):
-                relay_when_here(1, (t - 8) // 2)
+            if g == 0 and t in (3, 4, 6, 7):
+                relay_when_here(1, t // 6, t % 3)
             if g == 1 and t in (3, 4):
                 part_join(0, t - 3)
 

time: 60.1 us -> 60.1 us (level)
  the two profiles are of different devices: /device:TPU:69 before, /device:TPU:1 now
where the time goes in v3:
time: 60.1 us; the launch traced here: 60 us
  Pallas kernels  59.2 us (99%)
  between operations  0.8 us (1%)
    pallas_call x1, Pallas kernels, body(): pl.pallas_call(kernel, out_shape=(rows, rows, small, small), in_specs=[pl...  56.6 us
    pallas_call x1, Pallas kernels, body(): pl.pallas_call(hand_over, out_shape=(rows, rows, small, small), in_specs=...  2.62 us

profile of v3, /device:TPU:1, one launch (start us, length us, event | category | flops | bytes accessed | tf_op | source)
XLA Modules:
  0.0 60.0 jit_solution(8007272376601488573)
XLA Ops:
  0.6 56.6 %packed_attention.1 = (bf16[128,4096]{1,0:T(8,128)(2,1)}, bf16[128,4096]{1,0:T(8,128)(2,1)}, bf16[128,512]{1,0:T(8,128)(2,1)}, bf16[128,512]{1,0:T(8,128)(2,1)}) custom-call(s32[9]{0:T(128)} %bounds.1, bf16[128,4096]{1,0:T(8,128)(2,1)} %q_in.1, bf16[128,512]{1,0:T(8,128)(2,1)} %k_in.1, bf16[128,512]{1,0:T(8,128)(2,1)} %v_in.1, bf16[128,4096]{1,0:T(8,128)(2,1)} %g_in.1), custom_call_target="tpu_custom_call" | custom-call | tf_op jit(solution)/shard_map/packed_attention/pallas_call | solution.py:384
  57.2 2.6 %hand_over.1 = (bf16[128,4096]{1,0:T(8,128)(2,1)}, bf16[128,4096]{1,0:T(8,128)(2,1)}, bf16[128,512]{1,0:T(8,128)(2,1)}, bf16[128,512]{1,0:T(8,128)(2,1)}) custom-call(bf16[128,4096]{1,0:T(8,128)(2,1)} %get-tuple-element.8.refs_0_, bf16[128,4096]{1,0:T(8,128)(2,1)} %get-tuple-element.9.refs_1_, bf16[128,512]{1,0:T(8,128)(2,1)} %get-tuple-element.10.refs_2_, ...), custom_call_target="tpu_custom_call" | custom-call | tf_op jit(solution)/shard_map/hand_over/pallas_call | solution.py:416
